TPU v7x, 32 devices: a whole 2x2x4 slice. The times are simulated.
32 devices in a mesh: row: 8 (over z, x), col: 4 (over y, core).
Axes of the slice: x: 2, y: 2, z: 4, core: 2. Of those that a mesh axis runs over, the one named last changes fastest.
Arguments:
- source_points: float32 [3, 16384], P(None, 'row'), may hold values from -4 to 4
- target_points: float32 [3, 65536], P(None, 'col'), may hold values from -4 to 4
- source_potential: float32 [16384], P('row'), may hold values from -2.5 to 3.6
- target_potential: float32 [65536], P('col'), may hold values from -2.5 to 3.6
- neighbours: int32 [64, 64], P('row'), may hold values from -1 to 255, as said below
Outputs:
- source_dual: float32 [16384], P('row')
- target_dual: float32 [65536], P('col')
Inputs may be any that keep to these rules, and one draw needn't show every extreme that they name: `neighbours`: each row block lists, in increasing order, between 32 and 64 distinct column-block ids, then -1 up to 64 entries; some row block lists 64; every column block is listed by at least one row block.
All inputs are finite; a program needn't handle non-finite values.
Results may differ from a plain program's by a relative error of at most 0.0003.
Values sent between devices are 32-bit elements; how exact they have to be, the bound alone decides.
A program may use at most 64 MiB of HBM per device.

v0:
```python
import functools
import math

import jax
import jax.numpy as jnp
from jax import lax
from jax.experimental import pallas as pl
from jax.experimental.pallas import tpu as pltpu
from jax.sharding import PartitionSpec as P

BLOCK = 256
ITERS = 2
EPS = 0.02
SCALE = math.log2(math.e) / EPS
NEG = -1e30
UNROLL = 4
DEPTH = 48
VMEM = pltpu.VMEM
SMEM = pltpu.SMEM


def pieces(values):
    first = values.astype(jnp.bfloat16).astype(jnp.float32)
    rest = values - first
    second = rest.astype(jnp.bfloat16).astype(jnp.float32)
    return first, second, rest - second


def augmented(points, level, source):
    packed = jnp.concatenate([points, points], axis=0)
    place = lax.broadcasted_iota(jnp.int32, packed.shape, 0)
    squares = jnp.where(place < 3, packed * packed, 0.0)
    norm = jnp.sum(squares, axis=0, keepdims=True)
    level = SCALE * (level - 0.5 * norm)
    if source:
        level_at, one_at, coordinates = 3, 4, SCALE * packed
    else:
        level_at, one_at, coordinates = 4, 3, packed
    rows = jnp.where(
        place < 3,
        coordinates,
        jnp.where(place == level_at, level, jnp.where(place == one_at, 1.0, 0.0)),
    )
    a, b, c = pieces(rows)
    if source:
        return jnp.concatenate([a, a, b, b, a, c], axis=0)
    return jnp.concatenate([a, b, a, b, c, a], axis=0)


def slot_lse(scores):
    tiles = scores.reshape(scores.shape[0] // 8, 8, scores.shape[1])
    top = jnp.max(tiles, axis=0)
    return top, jnp.sum(jnp.exp2(tiles - top[None]), axis=0)


def merge(top_ref, mass_ref, at, top, mass):
    old = top_ref[at]
    new = jnp.maximum(old, top)
    top_ref[at] = new
    mass_ref[at] = mass_ref[at] * jnp.exp2(old - new) + mass * jnp.exp2(top - new)


def total(top, mass):
    peak = jnp.max(top, axis=1)
    amount = jnp.sum(mass * jnp.exp2(top - peak[:, None, :]), axis=1)
    return peak + jnp.log2(jnp.maximum(amount, 1e-30))


def sweep_kernel(
    count, row_list, col_list, source, f, target, g, row_out, g_out,
    x_all, xt_all, y_all, yt_all, row_top, row_mass, col_top, col_mass,
):
    rows, cols = f.shape[0], g.shape[0]

    def build(at, ref, level, straight, turned, is_source):
        per = ref.shape[2] // BLOCK
        lanes = pl.ds(pl.multiple_of(at % per * BLOCK, BLOCK), BLOCK)
        block = augmented(ref[at // per, :, lanes], level[at], is_source)
        turned[at] = block.astype(jnp.bfloat16)
        straight[at] = block.T.astype(jnp.bfloat16)

    @pl.loop(0, rows, unroll=4)
    def _(at):
        build(at, source, f, x_all, xt_all, True)

    for at in range(cols):
        build(at, target, g, y_all, yt_all, False)
    x_all[rows] = jnp.zeros_like(x_all[rows])
    xt_all[rows] = jnp.zeros_like(xt_all[rows])
    y_all[cols] = jnp.zeros_like(y_all[cols])
    yt_all[cols] = jnp.zeros_like(yt_all[cols])
    row_top[...] = jnp.full_like(row_top, NEG)
    row_mass[...] = jnp.zeros_like(row_mass)
    col_top[...] = jnp.full_like(col_top, NEG)
    col_mass[...] = jnp.zeros_like(col_mass)

    @pl.loop(0, (count[0] + UNROLL - 1) // UNROLL)
    def _(turn):
        found = []
        for lane in range(UNROLL):
            row = row_list[turn * UNROLL + lane]
            col = col_list[turn * UNROLL + lane]
            by_col = jnp.dot(x_all[row], yt_all[col], preferred_element_type=jnp.float32)
            by_row = jnp.dot(y_all[col], xt_all[row], preferred_element_type=jnp.float32)
            found.append((row, col, slot_lse(by_row), slot_lse(by_col)))
        for row, col, of_row, of_col in found:
            merge(row_top, row_mass, row, *of_row)
            merge(col_top, col_mass, col, *of_col)

    row_out[...] = total(row_top[:rows], row_mass[:rows])
    g_out[...] = g[:, 0, :] - total(col_top[:cols], col_mass[:cols]) / (2 * SCALE)


def sweep(count, row_list, col_list, source, f, target, g):
    f, g = f.reshape(-1, 1, BLOCK), g.reshape(-1, 1, BLOCK)
    rows, cols = f.shape[0], g.shape[0]
    bf16, f32 = jnp.bfloat16, jnp.float32
    return pl.pallas_call(
        sweep_kernel,
        out_shape=(
            jax.ShapeDtypeStruct((rows, BLOCK), f32),
            jax.ShapeDtypeStruct((cols, BLOCK), f32),
        ),
        in_specs=[pl.BlockSpec(memory_space=SMEM)] * 3 + [pl.BlockSpec(memory_space=VMEM)] * 4,
        out_specs=(pl.BlockSpec(memory_space=VMEM),) * 2,
        scratch_shapes=[
            VMEM((rows + 1, BLOCK, DEPTH), bf16),
            VMEM((rows + 1, DEPTH, BLOCK), bf16),
            VMEM((cols + 1, BLOCK, DEPTH), bf16),
            VMEM((cols + 1, DEPTH, BLOCK), bf16),
            VMEM((rows + 1, 8, BLOCK), f32),
            VMEM((rows + 1, 8, BLOCK), f32),
            VMEM((cols + 1, 8, BLOCK), f32),
            VMEM((cols + 1, 8, BLOCK), f32),
        ],
        compiler_params=pltpu.CompilerParams(vmem_limit_bytes=48 * 1024 * 1024),
    )(count, row_list, col_list, source, f, target, g)


def lse2(parts):
    peak = jnp.max(parts, axis=0)
    return peak + jnp.log2(jnp.sum(jnp.exp2(parts - peak[None]), axis=0))


def place_of(device, n_col):
    return (device // n_col, lax.rem(device, n_col))


def meet(peers):
    barrier = pltpu.get_barrier_semaphore()
    for amount, where in peers:

        @pl.loop(1, amount)
        def _(step):
            pl.semaphore_signal(
                barrier, inc=1, device_id=where(step), device_id_type=pl.DeviceIdType.MESH
            )

    pl.semaphore_wait(barrier, sum(amount - 1 for amount, _ in peers))


def remote(src, dst, send, recv, where):
    return pltpu.make_async_remote_copy(
        src_ref=src, dst_ref=dst, send_sem=send, recv_sem=recv,
        device_id=where, device_id_type=pl.DeviceIdType.MESH,
    )


def gather_kernel(
    n_row, n_col, spread, source, lists, target, source_out, lists_out, target_out,
    source_send, source_recv, lists_send, lists_recv, target_send, target_recv,
):
    row, col = lax.axis_index("row"), lax.axis_index("col")

    def by_row(step):
        return (lax.rem(row + step, n_row), col)

    def by_col(step):
        return (row, lax.rem(col + step, n_col))

    meet([(n_row, by_row)] + ([(n_col, by_col)] if spread else []))

    def copies(step):
        to = by_row(step)
        return (
            remote(source, source_out.at[row], source_send.at[step], source_recv.at[step], to),
            remote(lists, lists_out.at[row], lists_send.at[step], lists_recv.at[step], to),
        )

    def target_copy(step):
        to = by_col(step)
        return remote(
            target.at[to[1]], target_out.at[col], target_send.at[step], target_recv.at[step], to
        )

    @pl.loop(1, n_row)
    def _(step):
        for copy in copies(step):
            copy.start()

    if spread:

        @pl.loop(1, n_col)
        def _(step):
            target_copy(step).start()

        target_out[col] = target[col]

        @pl.loop(1, n_col)
        def _(step):
            target_copy(step).wait()
    else:
        target_out[...] = target[...]

    source_out[row] = source[...]
    lists_out[row] = lists[...]

    @pl.loop(1, n_row)
    def _(step):
        for copy in copies(step):
            copy.wait()


def gather(n_row, n_col, spread, source, lists, target):
    dma = pltpu.SemaphoreType.DMA
    return pl.pallas_call(
        functools.partial(gather_kernel, n_row, n_col, spread),
        out_shape=(
            jax.ShapeDtypeStruct((n_row,) + source.shape, source.dtype),
            jax.ShapeDtypeStruct((n_row,) + lists.shape, lists.dtype),
            jax.ShapeDtypeStruct(target.shape, target.dtype),
        ),
        in_specs=[pl.BlockSpec(memory_space=VMEM)] * 3,
        out_specs=(pl.BlockSpec(memory_space=VMEM),) * 3,
        scratch_shapes=[dma((n_row,))] * 4 + [dma((n_col,))] * 2,
        compiler_params=pltpu.CompilerParams(
            collective_id=0, has_side_effects=True, vmem_limit_bytes=32 * 1024 * 1024
        ),
    )(source, lists, target)


def exchange_kernel(n_row, n_col, spread, last, *refs):
    if last:
        (
            sums, f, g, f_out, g_out,
            parts, send, recv, f_send, f_recv, g_send, g_recv,
        ) = refs
    else:
        sums, f, f_out, parts, send, recv, f_send, f_recv = refs
    n_dev = n_row * n_col
    row, col = lax.axis_index("row"), lax.axis_index("col")
    me = row * n_col + col

    def anyone(step):
        return place_of(lax.rem(me + step, n_dev), n_col)

    def by_col(step):
        return (row, lax.rem(col + step, n_col))

    def by_row(step):
        return (lax.rem(row + step, n_row), col)

    meet([(n_dev, anyone)])

    def sum_copy(step):
        return remote(
            sums.at[lax.rem(me + step, n_dev)], parts.at[me],
            send.at[step], recv.at[step], anyone(step),
        )

    def g_copy(step):
        to = anyone(step) if spread else by_row(step)
        return remote(
            g.at[to[1] if spread else 0], g_out.at[me if spread else row],
            g_send.at[step], g_recv.at[step], to,
        )

    @pl.loop(1, n_dev)
    def _(step):
        sum_copy(step).start()

    parts[me] = sums[me]
    if last:

        @pl.loop(1, n_dev if spread else n_row)
        def _(step):
            g_copy(step).start()

        g_out[me if spread else row] = g[col if spread else 0]

    @pl.loop(1, n_dev)
    def _(step):
        sum_copy(step).wait()

    spot = col if last else me
    f_out[spot] = f[me] - lse2(parts[...]) / (2 * SCALE)
    amount, where = (n_col, by_col) if last else (n_dev, anyone)

    def f_copy(step):
        return remote(
            f_out.at[spot], f_out.at[spot], f_send.at[step], f_recv.at[step], where(step)
        )

    @pl.loop(1, amount)
    def _(step):
        f_copy(step).start()

    if last:

        @pl.loop(1, n_dev if spread else n_row)
        def _(step):
            g_copy(step).wait()

    @pl.loop(1, amount)
    def _(step):
        f_copy(step).wait()


def exchange(n_row, n_col, spread, last, sums, f, g):
    n_dev = n_row * n_col
    dma = pltpu.SemaphoreType.DMA
    sums, f = (a.reshape(n_dev, -1, 128) for a in (sums, f))
    amount = n_col if last else n_dev
    out = [jax.ShapeDtypeStruct((amount,) + f.shape[1:], f.dtype)]
    scratch = [VMEM(sums.shape, sums.dtype)] + [dma((n_dev,))] * 2 + [dma((amount,))] * 2
    args = [sums, f]
    if last:
        fan = n_dev if spread else n_row
        g = g.reshape(n_col if spread else 1, -1, 128)
        out.append(jax.ShapeDtypeStruct((fan,) + g.shape[1:], g.dtype))
        scratch += [dma((fan,))] * 2
        args.append(g)
    return pl.pallas_call(
        functools.partial(exchange_kernel, n_row, n_col, spread, last),
        out_shape=tuple(out),
        in_specs=[pl.BlockSpec(memory_space=VMEM)] * len(args),
        out_specs=(pl.BlockSpec(memory_space=VMEM),) * len(out),
        scratch_shapes=scratch,
        compiler_params=pltpu.CompilerParams(
            collective_id=2 if last else 1,
            has_side_effects=True,
            vmem_limit_bytes=32 * 1024 * 1024,
        ),
    )(*args)


def on_device(n_row, n_col, source_points, target_points, source_level, target_level, neighbours):
    group = target_points.shape[1] // BLOCK
    share = group // n_row
    spread = share % n_col == 0
    me_row, me_col = lax.axis_index("row"), lax.axis_index("col")
    start, length = me_row * share * BLOCK, share * BLOCK
    source = jnp.concatenate([source_points, source_level[None]], axis=0)
    target = jnp.concatenate(
        [
            lax.dynamic_slice_in_dim(target_points, start, length, 1),
            lax.dynamic_slice_in_dim(target_level, start, length, 0)[None],
        ],
        axis=0,
    )
    if spread:
        target = target.reshape(4, n_col, -1).transpose(1, 0, 2)
        part = share // n_col
        own = (
            jnp.arange(n_col)[:, None] * group
            + me_row * share + me_col * part + jnp.arange(part)[None, :]
        ).reshape(-1)
    else:
        target = target[None]
        own = me_col * group + me_row * share + jnp.arange(share)
    source, lists, target = gather(n_row, n_col, spread, source, neighbours, target)
    lists = lists.reshape(-1, lists.shape[-1])
    f, g = source[:, 3], target[:, 3]
    rows = lists.shape[0]
    cols = own.shape[0]
    capacity = rows * cols
    mask = jnp.any(lists[None] == own[:, None, None], axis=2).reshape(-1)
    order = jnp.arange(capacity)
    place = jnp.sum(jnp.where((order[None, :] <= order[:, None]) & mask[None, :], 1, 0), axis=1)
    count = place[-1:]
    hit = mask[None, :] & (place[None, :] == order[:, None] + 1)
    pick = jnp.sum(jnp.where(hit, order[None, :], 0), axis=1)
    live = order < count
    row_list = jnp.where(live, pick % rows, rows)
    col_list = jnp.where(live, pick // rows, cols)

    for turn in range(ITERS):
        sums, g = sweep(count, row_list, col_list, source, f, target, g)
        if turn < ITERS - 1:
            (f,) = exchange(n_row, n_col, spread, False, sums, f, None)
    f, g = exchange(n_row, n_col, spread, True, sums, f, g)
    return f.reshape(-1), g.reshape(-1)


def solution(mesh):
    return jax.shard_map(
        functools.partial(on_device, mesh.shape["row"], mesh.shape["col"]),
        mesh=mesh,
        in_specs=(P(None, "row"), P(None, "col"), P("row"), P("col"), P("row", None)),
        out_specs=(P("row"), P("col")),
        check_vma=False,
    )
```

profile of v0, /device:TPU:0, one launch (start us, length us, event | category | flops | bytes accessed | tf_op | source)
XLA Modules:
  0.0 86.8 jit_solution(9530187051339238139)
XLA Ops:
  0.6 0.0 copy-start
  0.7 0.1 iota_add_fusion.1
  0.7 0.1 add.72
  0.8 0.8 copy-done
  1.6 0.0 dynamic-slice-start
  1.6 0.7 dynamic-slice-done
  2.3 0.0 copy-start.2
  2.3 0.7 copy-done.2
  3.0 0.0 copy-done.3
  3.1 0.7 copy-done.1
  3.7 12.2 %shard_map.68 = (f32[8,4,2048]{2,1,0:T(4,128)S(1)}, s32[8,8,64]{2,1,0:T(8,128)S(1)}, f32[4,4,512]{2,1,0:T(4,128)S(1)}) custom-call(f32[4,2048]{1,0:T(4,128)S(1)} %pad_maximum_fusion.source, s32[8,64]{1,0:T(8,128)S(1)} %copy-done.1, f32[4,4,512]{2,1,0:T(4,128)S(1)} %maximum_bitcast_fusion.target), custom_call_target="tpu_custom_call" | custom-call | tf_op jit(solution)/shard_map/pallas_call | solution.py:226
  16.0 0.3 compare_reduce_fusion
  16.3 0.1 and.28
  16.3 0.2 select_reduce_fusion.1
  16.5 0.6 slice.9.count
  17.1 0.4 select_reduce_fusion
  17.5 0.7 fusion.2
  18.2 0.1 slice.10
  18.2 19.7 %shard_map.69 = (f32[64,256]{1,0:T(8,128)S(1)}, f32[8,256]{1,0:T(8,128)S(1)}) custom-call(s32[1]{0:T(128)} %slice.9.count, s32[512]{0:T(512)S(1)} %get-tuple-element.21.row_list, s32[512]{0:T(512)S(1)} %get-tuple-element.20.col_list, f32[8,4,2048]{2,1,0:T(4,128)S(1)} %get-tuple-element.12.source, f32[64,1,256]{2,1,0:T(1,128)S(1)} %bitcast.14, ...), custom_call_target="tpu_custom_call" | custom-call | tf_op jit(solution)/shard_map/pallas_call | solution.py:118
  38.0 16.3 %shard_map.70.refs_1_ = f32[32,4,128]{2,1,0:T(4,128)S(1)} custom-call(f32[32,4,128]{2,1,0:T(4,128)S(1)} %reshape.60.refs_0_, f32[32,4,128]{2,1,0:T(4,128)S(1)} %bitcast.15), custom_call_target="tpu_custom_call" | custom-call | tf_op jit(solution)/shard_map/pallas_call | solution.py:333
  54.3 19.7 %shard_map.71 = (f32[64,256]{1,0:T(8,128)S(1)}, f32[8,256]{1,0:T(8,128)S(1)}) custom-call(s32[1]{0:T(128)} %slice.9.count, s32[512]{0:T(512)S(1)} %get-tuple-element.21.row_list, s32[512]{0:T(512)S(1)} %get-tuple-element.20.col_list, f32[8,4,2048]{2,1,0:T(4,128)S(1)} %get-tuple-element.12.source, f32[64,1,256]{2,1,0:T(1,128)S(1)} %bitcast.13, ...), custom_call_target="tpu_custom_call" | custom-call | tf_op jit(solution)/shard_map/pallas_call | solution.py:118
  74.1 11.5 %shard_map.72 = (f32[4,4,128]{2,1,0:T(4,128)S(1)}, f32[32,4,128]{2,1,0:T(4,128)S(1)}) custom-call(f32[32,4,128]{2,1,0:T(4,128)S(1)} %reshape.63.refs_0_, f32[32,4,128]{2,1,0:T(4,128)S(1)} %shard_map.70.refs_1_, f32[4,4,128]{2,1,0:T(4,128)S(1)} %reshape.64.refs_2_), custom_call_target="tpu_custom_call" | custom-call | tf_op jit(solution)/shard_map/pallas_call | solution.py:333
  85.6 0.6 copy.9
  86.2 0.6 copy.10
  (12 shorter events, 0.1 us)
Async XLA Ops:
  0.6 1.0 %copy-start = (f32[3,16384]{1,0:T(4,128)S(1)}, f32[3,16384]{1,0:T(4,128)}, u32[]{:S(2)}) copy-start(f32[3,16384]{1,0:T(4,128)} %param.6) | copy-start | bytes 589828
  1.6 0.7 dynamic-slice-start
  2.3 0.8 copy-start.2
  2.3 0.8 copy-start.3
  3.0 0.7 copy-start.1
where the time goes:
time: 87.6 us; the launch traced here: 86.8 us
  Pallas kernels  79.4 us (91%)
  local copies, waits for them, and re-layouts  5.02 us (6%)
  other arithmetic  1.61 us (2%)
    pallas_call x2, Pallas kernels, sweep(): pl.pallas_call(sweep_kernel, out_shape=(jax.ShapeDtypeStruct((rows, BLOCK...  39.3 us
    pallas_call x2, Pallas kernels, exchange(): pl.pallas_call(functools.partial(exchange_kernel, n_row, n_col, spread, l...  27.9 us
    pallas_call x1, Pallas kernels, gather(): pl.pallas_call(functools.partial(gather_kernel, n_row, n_col, spread), ou...  12.2 us
    unnamed x10, local copies, waits for them, and re-layouts  3.41 us

commit v1 on v0

--- a/solution.py
+++ b/solution.py
@@ -13,7 +13,8 @@
 EPS = 0.02
 SCALE = math.log2(math.e) / EPS
 NEG = -1e30
-UNROLL = 4
+UNROLL = 8
+CUT = 4
 DEPTH = 48
 VMEM = pltpu.VMEM
 SMEM = pltpu.SMEM
@@ -48,9 +49,15 @@
 
 
 def slot_lse(scores):
-    tiles = scores.reshape(scores.shape[0] // 8, 8, scores.shape[1])
-    top = jnp.max(tiles, axis=0)
-    return top, jnp.sum(jnp.exp2(tiles - top[None]), axis=0)
+    depth = scores.shape[0] // CUT
+    tops, masses = [], []
+    for at in range(CUT):
+        tiles = scores[at * depth : (at + 1) * depth].reshape(depth // 8, 8, scores.shape[1])
+        top = jnp.max(tiles, axis=0)
+        tops.append(top)
+        masses.append(jnp.sum(jnp.exp2(tiles - top[None]), axis=0))
+    peak = functools.reduce(jnp.maximum, tops)
+    return peak, sum(mass * jnp.exp2(top - peak) for top, mass in zip(tops, masses))
 
 
 def merge(top_ref, mass_ref, at, top, mass):
@@ -67,7 +74,7 @@
 
 
 def sweep_kernel(
-    count, row_list, col_list, source, f, target, g, row_out, g_out,
+    pairs, source, f, target, g, row_out, g_out,
     x_all, xt_all, y_all, yt_all, row_top, row_mass, col_top, col_mass,
 ):
     rows, cols = f.shape[0], g.shape[0]
@@ -94,12 +101,12 @@
     col_top[...] = jnp.full_like(col_top, NEG)
     col_mass[...] = jnp.zeros_like(col_mass)
 
-    @pl.loop(0, (count[0] + UNROLL - 1) // UNROLL)
+    @pl.loop(0, (pairs[pairs.shape[0] - 1] + UNROLL - 1) // UNROLL)
     def _(turn):
         found = []
         for lane in range(UNROLL):
-            row = row_list[turn * UNROLL + lane]
-            col = col_list[turn * UNROLL + lane]
+            pair = pairs[turn * UNROLL + lane]
+            row, col = pair & 0xFFFF, pair >> 16
             by_col = jnp.dot(x_all[row], yt_all[col], preferred_element_type=jnp.float32)
             by_row = jnp.dot(y_all[col], xt_all[row], preferred_element_type=jnp.float32)
             found.append((row, col, slot_lse(by_row), slot_lse(by_col)))
@@ -111,7 +118,7 @@
     g_out[...] = g[:, 0, :] - total(col_top[:cols], col_mass[:cols]) / (2 * SCALE)
 
 
-def sweep(count, row_list, col_list, source, f, target, g):
+def sweep(pairs, source, f, target, g):
     f, g = f.reshape(-1, 1, BLOCK), g.reshape(-1, 1, BLOCK)
     rows, cols = f.shape[0], g.shape[0]
     bf16, f32 = jnp.bfloat16, jnp.float32
@@ -121,7 +128,7 @@
             jax.ShapeDtypeStruct((rows, BLOCK), f32),
             jax.ShapeDtypeStruct((cols, BLOCK), f32),
         ),
-        in_specs=[pl.BlockSpec(memory_space=SMEM)] * 3 + [pl.BlockSpec(memory_space=VMEM)] * 4,
+        in_specs=[pl.BlockSpec(memory_space=SMEM)] + [pl.BlockSpec(memory_space=VMEM)] * 4,
         out_specs=(pl.BlockSpec(memory_space=VMEM),) * 2,
         scratch_shapes=[
             VMEM((rows + 1, BLOCK, DEPTH), bf16),
@@ -134,7 +141,7 @@
             VMEM((cols + 1, 8, BLOCK), f32),
         ],
         compiler_params=pltpu.CompilerParams(vmem_limit_bytes=48 * 1024 * 1024),
-    )(count, row_list, col_list, source, f, target, g)
+    )(pairs, source, f, target, g)
 
 
 def lse2(parts):
@@ -377,15 +384,16 @@
     mask = jnp.any(lists[None] == own[:, None, None], axis=2).reshape(-1)
     order = jnp.arange(capacity)
     place = jnp.sum(jnp.where((order[None, :] <= order[:, None]) & mask[None, :], 1, 0), axis=1)
-    count = place[-1:]
-    hit = mask[None, :] & (place[None, :] == order[:, None] + 1)
-    pick = jnp.sum(jnp.where(hit, order[None, :], 0), axis=1)
-    live = order < count
-    row_list = jnp.where(live, pick % rows, rows)
-    col_list = jnp.where(live, pick // rows, cols)
+    count = jnp.max(place)
+    slot = jnp.arange(-(-capacity // UNROLL) * UNROLL + 1)
+    hit = mask[None, :] & (place[None, :] == slot[:, None] + 1)
+    code = order % rows + (order // rows) * 65536
+    pick = jnp.sum(jnp.where(hit, code[None, :], 0), axis=1)
+    pairs = jnp.where(slot < count, pick, rows + cols * 65536)
+    pairs = jnp.where(slot == slot.shape[0] - 1, count, pairs)
 
     for turn in range(ITERS):
-        sums, g = sweep(count, row_list, col_list, source, f, target, g)
+        sums, g = sweep(pairs, source, f, target, g)
         if turn < ITERS - 1:
             (f,) = exchange(n_row, n_col, spread, False, sums, f, None)
     f, g = exchange(n_row, n_col, spread, True, sums, f, g)

time: 87.6 us -> 80.8 us (0.922)
  Pallas kernels: 79.4 us -> 73.7 us
  local copies, waits for them, and re-layouts: 5.02 us -> 2.33 us
  other arithmetic: 1.61 us -> 3.03 us
    pallas_call x2, Pallas kernels: 39.3 us -> 29.6 us  [sweep(): pl.pallas_call(sweep_kernel, out_shape=(jax.ShapeDtypeStruct((rows, BLOCK...]
    pallas_call x2, Pallas kernels: 27.9 us -> 31.8 us  [exchange(): pl.pallas_call(functools.partial(exchange_kernel, n_row, n_col, spread, l...]
    unnamed x10 -> x6, local copies, waits for them, and re-layouts: 3.41 us -> 1.29 us
where the time goes in v1:
time: 80.8 us; the launch traced here: 79.9 us
  Pallas kernels  73.7 us (91%)
  other arithmetic  3.03 us (4%)
  local copies, waits for them, and re-layouts  2.33 us (3%)
    pallas_call x2, Pallas kernels, exchange(): pl.pallas_call(functools.partial(exchange_kernel, n_row, n_col, spread, l...  31.8 us
    pallas_call x2, Pallas kernels, sweep(): pl.pallas_call(sweep_kernel, out_shape=(jax.ShapeDtypeStruct((rows, BLOCK...  29.6 us
    pallas_call x1, Pallas kernels, gather(): pl.pallas_call(functools.partial(gather_kernel, n_row, n_col, spread), ou...  12.3 us

profile of v1, /device:TPU:0, one launch (start us, length us, event | category | flops | bytes accessed | tf_op | source)
XLA Modules:
  0.0 79.9 jit_solution(16049221972112926005)
XLA Ops:
  0.6 0.0 copy-start
  0.6 0.0 copy-start.1
  0.7 0.1 iota_add_fusion.1
  0.7 0.1 add.87
  0.8 0.7 dynamic_slice.7
  1.5 0.0 copy-done
  1.6 0.8 pad_maximum_fusion.source
  2.4 0.0 copy-done.1
  2.4 12.3 %shard_map.68 = (f32[8,4,2048]{2,1,0:T(4,128)S(1)}, s32[8,8,64]{2,1,0:T(8,128)S(1)}, f32[4,4,512]{2,1,0:T(4,128)S(1)}) custom-call(f32[4,2048]{1,0:T(4,128)S(1)} %pad_maximum_fusion.source, s32[8,64]{1,0:T(8,128)S(1)} %copy-done.1, f32[4,4,512]{2,1,0:T(4,128)S(1)} %maximum_bitcast_fusion.target), custom_call_target="tpu_custom_call" | custom-call | tf_op jit(solution)/shard_map/pallas_call | solution.py:233
  14.7 0.3 compare_reduce_fusion
  15.0 0.1 and.45
  15.1 0.2 select_reduce_fusion.1
  15.3 0.6 reduce_max.9
  15.9 0.4 select_reduce_fusion
  16.3 0.7 select_select_fusion.pairs
  17.0 0.1 slice.6
  17.0 14.8 %shard_map.69 = (f32[64,256]{1,0:T(8,128)S(1)}, f32[8,256]{1,0:T(8,128)S(1)}) custom-call(s32[513]{0:T(1024)S(1)} %select_select_fusion.pairs, f32[8,4,2048]{2,1,0:T(4,128)S(1)} %get-tuple-element.12.source, f32[64,1,256]{2,1,0:T(1,128)S(1)} %bitcast.13, f32[4,4,512]{2,1,0:T(4,128)S(1)} %get-tuple-element.13.target, f32[8,1,256]{2,1,0:T(1,128)S(1)} %bitcast.16), custom_call_target="tpu_custom_call" | custom-call | tf_op jit(solution)/shard_map/pallas_call | solution.py:125
  31.9 17.4 %shard_map.70.refs_1_ = f32[32,4,128]{2,1,0:T(4,128)S(1)} custom-call(f32[32,4,128]{2,1,0:T(4,128)S(1)} %reshape.82.refs_0_, f32[32,4,128]{2,1,0:T(4,128)S(1)} %bitcast.14), custom_call_target="tpu_custom_call" | custom-call | tf_op jit(solution)/shard_map/pallas_call | solution.py:340
  49.3 14.8 %shard_map.71 = (f32[64,256]{1,0:T(8,128)S(1)}, f32[8,256]{1,0:T(8,128)S(1)}) custom-call(s32[513]{0:T(1024)S(1)} %select_select_fusion.pairs, f32[8,4,2048]{2,1,0:T(4,128)S(1)} %get-tuple-element.12.source, f32[64,1,256]{2,1,0:T(1,128)S(1)} %bitcast.12, f32[4,4,512]{2,1,0:T(4,128)S(1)} %get-tuple-element.13.target, f32[8,1,256]{2,1,0:T(1,128)S(1)} %reshape.84.g), custom_call_target="tpu_custom_call" | custom-call | tf_op jit(solution)/shard_map/pallas_call | solution.py:125
  64.2 14.5 %shard_map.72 = (f32[4,4,128]{2,1,0:T(4,128)S(1)}, f32[32,4,128]{2,1,0:T(4,128)S(1)}) custom-call(f32[32,4,128]{2,1,0:T(4,128)S(1)} %reshape.85.refs_0_, f32[32,4,128]{2,1,0:T(4,128)S(1)} %shard_map.70.refs_1_, f32[4,4,128]{2,1,0:T(4,128)S(1)} %reshape.86.refs_2_), custom_call_target="tpu_custom_call" | custom-call | tf_op jit(solution)/shard_map/pallas_call | solution.py:340
  78.6 0.6 copy.9
  79.2 0.6 copy.10
  (10 shorter events, 0.1 us)
Async XLA Ops:
  0.6 1.0 %copy-start = (f32[3,16384]{1,0:T(4,128)S(1)}, f32[3,16384]{1,0:T(4,128)}, u32[]{:S(2)}) copy-start(f32[3,16384]{1,0:T(4,128)} %param.6) | copy-start | bytes 589828
  0.6 1.8 %copy-start.1 = (s32[8,64]{1,0:T(8,128)S(1)}, s32[8,64]{1,0:T(8,128)}, u32[]{:S(2)}) copy-start(s32[8,64]{1,0:T(8,128)} %lists.1) | copy-start | bytes 6148

commit v2 on v1

--- a/solution.py
+++ b/solution.py
@@ -149,8 +149,23 @@
     return peak + jnp.log2(jnp.sum(jnp.exp2(parts - peak[None]), axis=0))
 
 
-def place_of(device, n_col):
-    return (device // n_col, lax.rem(device, n_col))
+def wrap(value, size):
+    return jnp.where(value >= size, value - size, value)
+
+
+def settle(ref, amount, semaphore):
+    chunks = ref.at[pl.ds(0, amount)]
+    pltpu.make_async_copy(chunks, chunks, semaphore).wait()
+
+
+def each_peer(n_row, n_col, visit):
+    for col_step in range(1, n_col):
+        visit(0, col_step)
+
+    @pl.loop(1, n_row)
+    def _(row_step):
+        for col_step in range(n_col):
+            visit(row_step, col_step)
 
 
 def meet(peers):
@@ -258,69 +273,50 @@
     row, col = lax.axis_index("row"), lax.axis_index("col")
     me = row * n_col + col
 
-    def anyone(step):
-        return place_of(lax.rem(me + step, n_dev), n_col)
-
-    def by_col(step):
-        return (row, lax.rem(col + step, n_col))
-
-    def by_row(step):
-        return (lax.rem(row + step, n_row), col)
-
-    meet([(n_dev, anyone)])
-
-    def sum_copy(step):
-        return remote(
-            sums.at[lax.rem(me + step, n_dev)], parts.at[me],
-            send.at[step], recv.at[step], anyone(step),
+    def peer(row_step, col_step):
+        return wrap(row + row_step, n_row), wrap(col + col_step, n_col)
+
+    def greet(row_step, col_step):
+        pl.semaphore_signal(
+            barrier, inc=1, device_id=peer(row_step, col_step),
+            device_id_type=pl.DeviceIdType.MESH,
         )
 
-    def g_copy(step):
-        to = anyone(step) if spread else by_row(step)
-        return remote(
-            g.at[to[1] if spread else 0], g_out.at[me if spread else row],
-            g_send.at[step], g_recv.at[step], to,
-        )
-
-    @pl.loop(1, n_dev)
-    def _(step):
-        sum_copy(step).start()
-
+    def send_sum(row_step, col_step):
+        to = peer(row_step, col_step)
+        remote(sums.at[to[0] * n_col + to[1]], parts.at[me], send, recv, to).start()
+
+    def send_g(row_step, col_step):
+        to = peer(row_step, col_step)
+        remote(
+            g.at[to[1] if spread else 0], g_out.at[me if spread else row], g_send, g_recv, to
+        ).start()
+
+    def send_f(row_step, col_step):
+        remote(
+            f_out.at[spot], f_out.at[spot], f_send, f_recv, peer(row_step, col_step)
+        ).start()
+
+    barrier = pltpu.get_barrier_semaphore()
+    each_peer(n_row, n_col, greet)
+    pl.semaphore_wait(barrier, n_dev - 1)
+    each_peer(n_row, n_col, send_sum)
     parts[me] = sums[me]
     if last:
-
-        @pl.loop(1, n_dev if spread else n_row)
-        def _(step):
-            g_copy(step).start()
-
+        each_peer(n_row, n_col if spread else 1, send_g)
         g_out[me if spread else row] = g[col if spread else 0]
-
-    @pl.loop(1, n_dev)
-    def _(step):
-        sum_copy(step).wait()
-
+    settle(parts, n_dev - 1, recv)
     spot = col if last else me
     f_out[spot] = f[me] - lse2(parts[...]) / (2 * SCALE)
-    amount, where = (n_col, by_col) if last else (n_dev, anyone)
-
-    def f_copy(step):
-        return remote(
-            f_out.at[spot], f_out.at[spot], f_send.at[step], f_recv.at[step], where(step)
-        )
-
-    @pl.loop(1, amount)
-    def _(step):
-        f_copy(step).start()
-
+    each_peer(1 if last else n_row, n_col, send_f)
+    settle(parts, n_dev - 1, send)
     if last:
-
-        @pl.loop(1, n_dev if spread else n_row)
-        def _(step):
-            g_copy(step).wait()
-
-    @pl.loop(1, amount)
-    def _(step):
-        f_copy(step).wait()
+        others = (n_dev if spread else n_row) - 1
+        settle(g_out, others, g_send)
+        settle(g_out, others, g_recv)
+    others = (n_col if last else n_dev) - 1
+    settle(f_out, others, f_send)
+    settle(f_out, others, f_recv)
 
 
 def exchange(n_row, n_col, spread, last, sums, f, g):
@@ -329,13 +325,13 @@
     sums, f = (a.reshape(n_dev, -1, 128) for a in (sums, f))
     amount = n_col if last else n_dev
     out = [jax.ShapeDtypeStruct((amount,) + f.shape[1:], f.dtype)]
-    scratch = [VMEM(sums.shape, sums.dtype)] + [dma((n_dev,))] * 2 + [dma((amount,))] * 2
+    scratch = [VMEM(sums.shape, sums.dtype)] + [dma] * 4
     args = [sums, f]
     if last:
         fan = n_dev if spread else n_row
         g = g.reshape(n_col if spread else 1, -1, 128)
         out.append(jax.ShapeDtypeStruct((fan,) + g.shape[1:], g.dtype))
-        scratch += [dma((fan,))] * 2
+        scratch += [dma] * 2
         args.append(g)
     return pl.pallas_call(
         functools.partial(exchange_kernel, n_row, n_col, spread, last),

time: 80.8 us -> 77.7 us (0.962)
  Pallas kernels: 73.7 us -> 70.9 us
    pallas_call x2, Pallas kernels: 31.8 us -> 27 us  [exchange(): pl.pallas_call(functools.partial(exchange_kernel, n_row, n_col, spread, l...]
    pallas_call x2, Pallas kernels: 29.6 us -> 31.6 us  [sweep(): pl.pallas_call(sweep_kernel, out_shape=(jax.ShapeDtypeStruct((rows, BLOCK...]
where the time goes in v2:
time: 77.7 us; the launch traced here: 77 us
  Pallas kernels  70.9 us (91%)
  other arithmetic  3.03 us (4%)
  local copies, waits for them, and re-layouts  2.33 us (3%)
    pallas_call x2, Pallas kernels, sweep(): pl.pallas_call(sweep_kernel, out_shape=(jax.ShapeDtypeStruct((rows, BLOCK...  31.6 us
    pallas_call x2, Pallas kernels, exchange(): pl.pallas_call(functools.partial(exchange_kernel, n_row, n_col, spread, l...  27 us
    pallas_call x1, Pallas kernels, gather(): pl.pallas_call(functools.partial(gather_kernel, n_row, n_col, spread), ou...  12.3 us

profile of v2, /device:TPU:0, one launch (start us, length us, event | category | flops | bytes accessed | tf_op | source)
XLA Modules:
  0.0 77.0 jit_solution(5038799573345427909)
XLA Ops:
  0.6 0.0 copy-start
  0.6 0.0 copy-start.1
  0.7 0.1 iota_add_fusion.1
  0.7 0.1 add.87
  0.8 0.7 dynamic_slice.7
  1.5 0.0 copy-done
  1.6 0.8 %pad_maximum_fusion.source = f32[4,2048]{1,0:T(4,128)S(1)} fusion(f32[1,2048]{1,0:T(1,128)} %bitcast.21, f32[3,2048]{1,0:T(4,128)} %param.5), kind=kLoop, calls=%fused_computation.5 | loop fusion | flops 8192 | bytes 65536 | tf_op jit(solution)/shard_map/concatenate | solution.py:356
  2.4 0.0 copy-done.1
  2.4 12.3 %shard_map.68 = (f32[8,4,2048]{2,1,0:T(4,128)S(1)}, s32[8,8,64]{2,1,0:T(8,128)S(1)}, f32[4,4,512]{2,1,0:T(4,128)S(1)}) custom-call(f32[4,2048]{1,0:T(4,128)S(1)} %pad_maximum_fusion.source, s32[8,64]{1,0:T(8,128)S(1)} %copy-done.1, f32[4,4,512]{2,1,0:T(4,128)S(1)} %maximum_bitcast_fusion.target), custom_call_target="tpu_custom_call" | custom-call | tf_op jit(solution)/shard_map/pallas_call | solution.py:248
  14.7 0.3 compare_reduce_fusion
  15.0 0.1 and.45
  15.1 0.2 select_reduce_fusion.1
  15.3 0.6 reduce_max.9
  15.9 0.4 select_reduce_fusion
  16.3 0.7 select_select_fusion.pairs
  17.0 0.1 slice.6
  17.0 15.8 %shard_map.69 = (f32[64,256]{1,0:T(8,128)S(1)}, f32[8,256]{1,0:T(8,128)S(1)}) custom-call(s32[513]{0:T(1024)S(1)} %select_select_fusion.pairs, f32[8,4,2048]{2,1,0:T(4,128)S(1)} %get-tuple-element.12.source, f32[64,1,256]{2,1,0:T(1,128)S(1)} %bitcast.13, f32[4,4,512]{2,1,0:T(4,128)S(1)} %get-tuple-element.13.target, f32[8,1,256]{2,1,0:T(1,128)S(1)} %bitcast.16), custom_call_target="tpu_custom_call" | custom-call | tf_op jit(solution)/shard_map/pallas_call | solution.py:125
  32.9 16.1 %shard_map.70.refs_1_ = f32[32,4,128]{2,1,0:T(4,128)S(1)} custom-call(f32[32,4,128]{2,1,0:T(4,128)S(1)} %reshape.82.refs_0_, f32[32,4,128]{2,1,0:T(4,128)S(1)} %bitcast.14), custom_call_target="tpu_custom_call" | custom-call | tf_op jit(solution)/shard_map/pallas_call | solution.py:336
  49.0 15.8 %shard_map.71 = (f32[64,256]{1,0:T(8,128)S(1)}, f32[8,256]{1,0:T(8,128)S(1)}) custom-call(s32[513]{0:T(1024)S(1)} %select_select_fusion.pairs, f32[8,4,2048]{2,1,0:T(4,128)S(1)} %get-tuple-element.12.source, f32[64,1,256]{2,1,0:T(1,128)S(1)} %bitcast.12, f32[4,4,512]{2,1,0:T(4,128)S(1)} %get-tuple-element.13.target, f32[8,1,256]{2,1,0:T(1,128)S(1)} %reshape.84.g), custom_call_target="tpu_custom_call" | custom-call | tf_op jit(solution)/shard_map/pallas_call | solution.py:125
  64.9 10.9 %shard_map.72 = (f32[4,4,128]{2,1,0:T(4,128)S(1)}, f32[32,4,128]{2,1,0:T(4,128)S(1)}) custom-call(f32[32,4,128]{2,1,0:T(4,128)S(1)} %reshape.85.refs_0_, f32[32,4,128]{2,1,0:T(4,128)S(1)} %shard_map.70.refs_1_, f32[4,4,128]{2,1,0:T(4,128)S(1)} %reshape.86.refs_2_), custom_call_target="tpu_custom_call" | custom-call | tf_op jit(solution)/shard_map/pallas_call | solution.py:336
  75.8 0.6 copy.9
  76.4 0.6 copy.10
  (10 shorter events, 0.1 us)
Async XLA Ops:
  0.6 1.0 %copy-start = (f32[3,16384]{1,0:T(4,128)S(1)}, f32[3,16384]{1,0:T(4,128)}, u32[]{:S(2)}) copy-start(f32[3,16384]{1,0:T(4,128)} %param.6) | copy-start | bytes 589828
  0.6 1.8 %copy-start.1 = (s32[8,64]{1,0:T(8,128)S(1)}, s32[8,64]{1,0:T(8,128)}, u32[]{:S(2)}) copy-start(s32[8,64]{1,0:T(8,128)} %lists.1) | copy-start | bytes 6148

commit v3 on v2

--- a/solution.py
+++ b/solution.py
@@ -106,7 +106,7 @@
         found = []
         for lane in range(UNROLL):
             pair = pairs[turn * UNROLL + lane]
-            row, col = pair & 0xFFFF, pair >> 16
+            row, col = pair & 0xFFFF, (pair >> 16) - 1
             by_col = jnp.dot(x_all[row], yt_all[col], preferred_element_type=jnp.float32)
             by_row = jnp.dot(y_all[col], xt_all[row], preferred_element_type=jnp.float32)
             found.append((row, col, slot_lse(by_row), slot_lse(by_col)))
@@ -380,13 +380,12 @@
     mask = jnp.any(lists[None] == own[:, None, None], axis=2).reshape(-1)
     order = jnp.arange(capacity)
     place = jnp.sum(jnp.where((order[None, :] <= order[:, None]) & mask[None, :], 1, 0), axis=1)
-    count = jnp.max(place)
-    slot = jnp.arange(-(-capacity // UNROLL) * UNROLL + 1)
-    hit = mask[None, :] & (place[None, :] == slot[:, None] + 1)
-    code = order % rows + (order // rows) * 65536
-    pick = jnp.sum(jnp.where(hit, code[None, :], 0), axis=1)
-    pairs = jnp.where(slot < count, pick, rows + cols * 65536)
-    pairs = jnp.where(slot == slot.shape[0] - 1, count, pairs)
+    slot = jnp.arange(-(-capacity // UNROLL) * UNROLL + 1)[:, None]
+    final = slot == slot.shape[0] - 1
+    hit = mask[None, :] & ((place[None, :] == slot + 1) | final)
+    code = order % rows + (order // rows + 1) * 65536
+    pick = jnp.sum(jnp.where(hit, jnp.where(final, 1, code[None, :]), 0), axis=1)
+    pairs = jnp.where(pick == 0, rows + (cols + 1) * 65536, pick)
 
     for turn in range(ITERS):
         sums, g = sweep(pairs, source, f, target, g)

time: 77.7 us -> 75.5 us (0.972); the launches traced: 77 us -> 76 us
  other arithmetic: 3.03 us -> 1.91 us
    pallas_call x2, Pallas kernels: 31.6 us -> 33.1 us  [sweep(): pl.pallas_call(sweep_kernel, out_shape=(jax.ShapeDtypeStruct((rows, BLOCK...]
    pallas_call x2, Pallas kernels: 27 us -> 25.6 us  [exchange(): pl.pallas_call(functools.partial(exchange_kernel, n_row, n_col, spread, l...]
where the time goes in v3:
time: 75.5 us; the launch traced here: 76 us
  Pallas kernels  71 us (94%)
  local copies, waits for them, and re-layouts  2.32 us (3%)
  other arithmetic  1.91 us (3%)
  between operations  0.77 us (1%)
    pallas_call x2, Pallas kernels, sweep(): pl.pallas_call(sweep_kernel, out_shape=(jax.ShapeDtypeStruct((rows, BLOCK...  33.1 us
    pallas_call x2, Pallas kernels, exchange(): pl.pallas_call(functools.partial(exchange_kernel, n_row, n_col, spread, l...  25.6 us
    pallas_call x1, Pallas kernels, gather(): pl.pallas_call(functools.partial(gather_kernel, n_row, n_col, spread), ou...  12.3 us

profile of v3, /device:TPU:0, one launch (start us, length us, event | category | flops | bytes accessed | tf_op | source)
XLA Modules:
  0.0 76.0 jit_solution(10924266296628899192)
XLA Ops:
  0.6 0.0 copy-start
  0.6 0.0 copy-start.1
  0.7 0.1 iota_add_fusion.1
  0.8 0.1 add.95
  0.9 0.7 dynamic_slice.7
  1.6 0.0 copy-done
  1.6 0.8 %pad_maximum_fusion.source = f32[4,2048]{1,0:T(4,128)S(1)} fusion(f32[1,2048]{1,0:T(1,128)} %bitcast.21, f32[3,2048]{1,0:T(4,128)} %param.5), kind=kLoop, calls=%fused_computation.5 | loop fusion | flops 8192 | bytes 65536 | tf_op jit(solution)/shard_map/concatenate | solution.py:356
  2.4 0.0 copy-done.1
  2.4 12.3 %shard_map.68 = (f32[8,4,2048]{2,1,0:T(4,128)S(1)}, s32[8,8,64]{2,1,0:T(8,128)S(1)}, f32[4,4,512]{2,1,0:T(4,128)S(1)}) custom-call(f32[4,2048]{1,0:T(4,128)S(1)} %pad_maximum_fusion.source, s32[8,64]{1,0:T(8,128)S(1)} %copy-done.1, f32[4,4,512]{2,1,0:T(4,128)S(1)} %maximum_bitcast_fusion.target), custom_call_target="tpu_custom_call" | custom-call | tf_op jit(solution)/shard_map/pallas_call | solution.py:248
  14.7 0.3 compare_reduce_fusion
  15.0 0.1 and.45
  15.1 0.2 select_reduce_fusion.1
  15.3 0.5 select_reduce_fusion
  15.8 0.1 slice.6
  15.9 16.6 %shard_map.69 = (f32[64,256]{1,0:T(8,128)S(1)}, f32[8,256]{1,0:T(8,128)S(1)}) custom-call(s32[513]{0:T(1024)S(1)} %compare_select_fusion.pairs, f32[8,4,2048]{2,1,0:T(4,128)S(1)} %get-tuple-element.12.source, f32[64,1,256]{2,1,0:T(1,128)S(1)} %bitcast.13, f32[4,4,512]{2,1,0:T(4,128)S(1)} %get-tuple-element.13.target, f32[8,1,256]{2,1,0:T(1,128)S(1)} %bitcast.16), custom_call_target="tpu_custom_call" | custom-call | tf_op jit(solution)/shard_map/pallas_call | solution.py:125
  32.5 15.1 %shard_map.70.refs_1_ = f32[32,4,128]{2,1,0:T(4,128)S(1)} custom-call(f32[32,4,128]{2,1,0:T(4,128)S(1)} %reshape.88.refs_0_, f32[32,4,128]{2,1,0:T(4,128)S(1)} %bitcast.14), custom_call_target="tpu_custom_call" | custom-call | tf_op jit(solution)/shard_map/pallas_call | solution.py:336
  47.6 16.6 %shard_map.71 = (f32[64,256]{1,0:T(8,128)S(1)}, f32[8,256]{1,0:T(8,128)S(1)}) custom-call(s32[513]{0:T(1024)S(1)} %compare_select_fusion.pairs, f32[8,4,2048]{2,1,0:T(4,128)S(1)} %get-tuple-element.12.source, f32[64,1,256]{2,1,0:T(1,128)S(1)} %bitcast.12, f32[4,4,512]{2,1,0:T(4,128)S(1)} %get-tuple-element.13.target, f32[8,1,256]{2,1,0:T(1,128)S(1)} %reshape.90.g), custom_call_target="tpu_custom_call" | custom-call | tf_op jit(solution)/shard_map/pallas_call | solution.py:125
  64.2 10.5 %shard_map.72 = (f32[4,4,128]{2,1,0:T(4,128)S(1)}, f32[32,4,128]{2,1,0:T(4,128)S(1)}) custom-call(f32[32,4,128]{2,1,0:T(4,128)S(1)} %reshape.91.refs_0_, f32[32,4,128]{2,1,0:T(4,128)S(1)} %shard_map.70.refs_1_, f32[4,4,128]{2,1,0:T(4,128)S(1)} %reshape.92.refs_2_), custom_call_target="tpu_custom_call" | custom-call | tf_op jit(solution)/shard_map/pallas_call | solution.py:336
  74.7 0.6 copy.9
  75.3 0.6 copy.10
  (12 shorter events, 0.1 us)
Async XLA Ops:
  0.6 1.0 %copy-start = (f32[3,16384]{1,0:T(4,128)S(1)}, f32[3,16384]{1,0:T(4,128)}, u32[]{:S(2)}) copy-start(f32[3,16384]{1,0:T(4,128)} %param.6) | copy-start | bytes 589828
  0.6 1.8 %copy-start.1 = (s32[8,64]{1,0:T(8,128)S(1)}, s32[8,64]{1,0:T(8,128)}, u32[]{:S(2)}) copy-start(s32[8,64]{1,0:T(8,128)} %lists.1) | copy-start | bytes 6148

commit v4 on v2

--- a/solution.py
+++ b/solution.py
@@ -191,6 +191,7 @@
 def gather_kernel(
     n_row, n_col, spread, source, lists, target, source_out, lists_out, target_out,
     source_send, source_recv, lists_send, lists_recv, target_send, target_recv,
+    pair_send, pair_recv,
 ):
     row, col = lax.axis_index("row"), lax.axis_index("col")
 
@@ -200,12 +201,17 @@
     def by_col(step):
         return (row, lax.rem(col + step, n_col))
 
-    meet([(n_row, by_row)] + ([(n_col, by_col)] if spread else []))
+    def sibling(step):
+        return (row, col + 1 - 2 * lax.rem(col, 2))
+
+    half = source.shape[1] // 2
+    lanes = pl.ds(pl.multiple_of(lax.rem(col, 2) * half, 128), half)
+    meet([(n_row, by_row), (n_col, by_col) if spread else (2, sibling)])
 
     def copies(step):
         to = by_row(step)
         return (
-            remote(source, source_out.at[row], source_send.at[step], source_recv.at[step], to),
+            remote(source.at[:, lanes], source_out.at[row, :, lanes], source_send.at[step], source_recv.at[step], to),
             remote(lists, lists_out.at[row], lists_send.at[step], lists_recv.at[step], to),
         )
 
@@ -234,13 +240,18 @@
     else:
         target_out[...] = target[...]
 
-    source_out[row] = source[...]
+    source_out[row, :, lanes] = source[:, lanes]
     lists_out[row] = lists[...]
 
     @pl.loop(1, n_row)
     def _(step):
         for copy in copies(step):
             copy.wait()
+
+    mine = source_out.at[:, :, lanes]
+    pair = remote(mine, mine, pair_send, pair_recv, sibling(1))
+    pair.start()
+    pair.wait()
 
 
 def gather(n_row, n_col, spread, source, lists, target):
@@ -254,7 +265,7 @@
         ),
         in_specs=[pl.BlockSpec(memory_space=VMEM)] * 3,
         out_specs=(pl.BlockSpec(memory_space=VMEM),) * 3,
-        scratch_shapes=[dma((n_row,))] * 4 + [dma((n_col,))] * 2,
+        scratch_shapes=[dma((n_row,))] * 4 + [dma((n_col,))] * 2 + [dma] * 2,
         compiler_params=pltpu.CompilerParams(
             collective_id=0, has_side_effects=True, vmem_limit_bytes=32 * 1024 * 1024
         ),

time: 77.7 us -> 76.1 us (0.979)
  Pallas kernels: 70.9 us -> 69.1 us
    pallas_call x2, Pallas kernels: 27 us -> 24.3 us  [exchange(): pl.pallas_call(functools.partial(exchange_kernel, n_row, n_col, spread, l...]
    pallas_call x2, Pallas kernels: 31.6 us -> 33.6 us  [sweep(): pl.pallas_call(sweep_kernel, out_shape=(jax.ShapeDtypeStruct((rows, BLOCK...]
    pallas_call x1, Pallas kernels: 12.3 us -> 11.2 us  [gather(): pl.pallas_call(functools.partial(gather_kernel, n_row, n_col, spread), ou...]
where the time goes in v4:
time: 76.1 us; the launch traced here: 75.3 us
  Pallas kernels  69.1 us (91%)
  other arithmetic  3.03 us (4%)
  local copies, waits for them, and re-layouts  2.33 us (3%)
  between operations  0.77 us (1%)
    pallas_call x2, Pallas kernels, sweep(): pl.pallas_call(sweep_kernel, out_shape=(jax.ShapeDtypeStruct((rows, BLOCK...  33.6 us
    pallas_call x2, Pallas kernels, exchange(): pl.pallas_call(functools.partial(exchange_kernel, n_row, n_col, spread, l...  24.3 us
    pallas_call x1, Pallas kernels, gather(): pl.pallas_call(functools.partial(gather_kernel, n_row, n_col, spread), ou...  11.2 us

profile of v4, /device:TPU:0, one launch (start us, length us, event | category | flops | bytes accessed | tf_op | source)
XLA Modules:
  0.0 75.3 jit_solution(15429528915223156334)
XLA Ops:
  0.6 0.0 copy-start
  0.6 0.0 copy-start.1
  0.7 0.1 iota_add_fusion.1
  0.7 0.1 add.87
  0.8 0.7 dynamic_slice.7
  1.5 0.0 copy-done
  1.6 0.8 %pad_maximum_fusion.source = f32[4,2048]{1,0:T(4,128)S(1)} fusion(f32[1,2048]{1,0:T(1,128)} %bitcast.21, f32[3,2048]{1,0:T(4,128)} %param.5), kind=kLoop, calls=%fused_computation.5 | loop fusion | flops 8192 | bytes 65536 | tf_op jit(solution)/shard_map/concatenate | solution.py:367
  2.4 0.0 copy-done.1
  2.4 11.2 %shard_map.68 = (f32[8,4,2048]{2,1,0:T(4,128)S(1)}, s32[8,8,64]{2,1,0:T(8,128)S(1)}, f32[4,4,512]{2,1,0:T(4,128)S(1)}) custom-call(f32[4,2048]{1,0:T(4,128)S(1)} %pad_maximum_fusion.source, s32[8,64]{1,0:T(8,128)S(1)} %copy-done.1, f32[4,4,512]{2,1,0:T(4,128)S(1)} %maximum_bitcast_fusion.target), custom_call_target="tpu_custom_call" | custom-call | tf_op jit(solution)/shard_map/pallas_call | solution.py:259
  13.6 0.3 compare_reduce_fusion
  13.9 0.1 and.45
  14.0 0.2 select_reduce_fusion.1
  14.2 0.6 reduce_max.9
  14.8 0.4 select_reduce_fusion
  15.2 0.7 select_select_fusion.pairs
  15.9 0.1 slice.6
  15.9 16.8 %shard_map.69 = (f32[64,256]{1,0:T(8,128)S(1)}, f32[8,256]{1,0:T(8,128)S(1)}) custom-call(s32[513]{0:T(1024)S(1)} %select_select_fusion.pairs, f32[8,4,2048]{2,1,0:T(4,128)S(1)} %get-tuple-element.12.source, f32[64,1,256]{2,1,0:T(1,128)S(1)} %bitcast.13, f32[4,4,512]{2,1,0:T(4,128)S(1)} %get-tuple-element.13.target, f32[8,1,256]{2,1,0:T(1,128)S(1)} %bitcast.16), custom_call_target="tpu_custom_call" | custom-call | tf_op jit(solution)/shard_map/pallas_call | solution.py:125
  32.8 14.6 %shard_map.70.refs_1_ = f32[32,4,128]{2,1,0:T(4,128)S(1)} custom-call(f32[32,4,128]{2,1,0:T(4,128)S(1)} %reshape.82.refs_0_, f32[32,4,128]{2,1,0:T(4,128)S(1)} %bitcast.14), custom_call_target="tpu_custom_call" | custom-call | tf_op jit(solution)/shard_map/pallas_call | solution.py:347
  47.4 16.8 %shard_map.71 = (f32[64,256]{1,0:T(8,128)S(1)}, f32[8,256]{1,0:T(8,128)S(1)}) custom-call(s32[513]{0:T(1024)S(1)} %select_select_fusion.pairs, f32[8,4,2048]{2,1,0:T(4,128)S(1)} %get-tuple-element.12.source, f32[64,1,256]{2,1,0:T(1,128)S(1)} %bitcast.12, f32[4,4,512]{2,1,0:T(4,128)S(1)} %get-tuple-element.13.target, f32[8,1,256]{2,1,0:T(1,128)S(1)} %reshape.84.g), custom_call_target="tpu_custom_call" | custom-call | tf_op jit(solution)/shard_map/pallas_call | solution.py:125
  64.3 9.7 %shard_map.72 = (f32[4,4,128]{2,1,0:T(4,128)S(1)}, f32[32,4,128]{2,1,0:T(4,128)S(1)}) custom-call(f32[32,4,128]{2,1,0:T(4,128)S(1)} %reshape.85.refs_0_, f32[32,4,128]{2,1,0:T(4,128)S(1)} %shard_map.70.refs_1_, f32[4,4,128]{2,1,0:T(4,128)S(1)} %reshape.86.refs_2_), custom_call_target="tpu_custom_call" | custom-call | tf_op jit(solution)/shard_map/pallas_call | solution.py:347
  74.0 0.6 copy.9
  74.6 0.6 copy.10
  (10 shorter events, 0.1 us)
Async XLA Ops:
  0.6 1.0 %copy-start = (f32[3,16384]{1,0:T(4,128)S(1)}, f32[3,16384]{1,0:T(4,128)}, u32[]{:S(2)}) copy-start(f32[3,16384]{1,0:T(4,128)} %param.6) | copy-start | bytes 589828
  0.6 1.8 %copy-start.1 = (s32[8,64]{1,0:T(8,128)S(1)}, s32[8,64]{1,0:T(8,128)}, u32[]{:S(2)}) copy-start(s32[8,64]{1,0:T(8,128)} %lists.1) | copy-start | bytes 6148
